TPU v7x, 512 devices: a whole 4x4x16 slice. The times are simulated.
512 devices in a mesh: lon: 64 (over y, z_lo, core), rad: 8 (over z_hi, x).
Axes of the slice: x: 4, y: 4, z: 16 (z_hi: 2, z_lo: 8; z = z_hi * 8 + z_lo), core: 2. Of those that a mesh axis runs over, the one named last changes fastest.
Arguments:
- logvisc: float32 [96, 256, 512], P('rad', 'lon'), may hold values from -1 to 1
- momentum: float32 [96, 256, 512], P('rad', 'lon'), may hold values from -6 to 6
- displacement: float32 [3, 96, 256, 512], P(None, 'rad', 'lon'), may hold values from -6 to 6
- ice_history: float32 [8, 256, 512], P(None, 'lon'), may hold values from -6 to 6
- load_steps: int32 [2], replicated, may hold values from 0 to 7
- site_cells: int32 [768], P('lon'), may hold values from 0 to 131071
- observed: float32 [3, 768], P(None, 'lon'), may hold values from -6 to 6
- site_weight: float32 [3, 768], P(None, 'lon'), may hold values from 2 to 6
Outputs:
- new_logvisc: float32 [96, 256, 512], P('rad', 'lon')
- half_momentum: float32 [96, 256, 512], P('rad', 'lon')
- misfit: float32 [1], replicated
Inputs may be any that keep to these rules, and one draw needn't show every extreme that they name: site_cells holds lon * 512 + lat of the surface cell where the site stands. load_steps indexes the first dimension of ice_history.
All inputs are finite; a program needn't handle non-finite values.
Results may differ from a plain program's by a relative error of at most 0.0003.
Values sent between devices are 32-bit elements; how exact they have to be, the bound alone decides.
A program may use at most 64 MiB of HBM per device.

v0:
```python
import math
import jax
import jax.numpy as jnp
from jax import lax
from jax.sharding import PartitionSpec as P

RELAX = 2
RELAX_RATE = 0.05
KERNEL_WIDTH = 0.1
KERNEL_WAVE = 40.0
PRIOR_WEIGHT = 0.1
LOAD_FACTOR = 1.0


def extended(block, sides, width, periodic):
    for axis, dim in sides:
        count = lax.axis_size(axis)
        forward = [(i, i + 1) for i in range(count - 1)]
        if periodic:
            forward.append((count - 1, 0))
        backward = [(target, source) for source, target in forward]
        low = lax.ppermute(
            lax.slice_in_dim(block, block.shape[dim] - width, None, axis=dim), axis, forward
        )
        high = lax.ppermute(lax.slice_in_dim(block, 0, width, axis=dim), axis, backward)
        block = jnp.concatenate([low, block, high], axis=dim)
    return block


def harmonic(center_fluid, other_fluid):
    summed = center_fluid + other_fluid
    coeff = 2.0 * center_fluid * other_fluid / summed
    slope = 2.0 * other_fluid * other_fluid / (summed * summed)
    return (coeff, slope)


def neighbours(padded):
    return [
        padded[:, 2:, 1:-1, 1:-1],
        padded[:, :-2, 1:-1, 1:-1],
        padded[:, 1:-1, 2:, 1:-1],
        padded[:, 1:-1, :-2, 1:-1],
        padded[:, 1:-1, 1:-1, 2:],
        padded[:, 1:-1, 1:-1, :-2],
    ]


def middle(padded):
    return padded[:, 1:-1, 1:-1, 1:-1]


def apply_operator(field_pad, fluid_pad):
    fluid_mid = middle(fluid_pad)
    field_mid = middle(field_pad)
    total = jnp.zeros(field_mid.shape, jnp.float32)
    for fluid_side, field_side in zip(neighbours(fluid_pad), neighbours(field_pad)):
        coeff, slope = harmonic(fluid_mid, fluid_side)
        total = total + coeff * (field_side - field_mid)
    return total


def fluid_gradient(state_pad, adjoint_pad, fluid_pad):
    fluid_mid = middle(fluid_pad)
    state_mid = middle(state_pad)
    adjoint_mid = middle(adjoint_pad)
    total = jnp.zeros(fluid_mid.shape, jnp.float32)
    for fluid_side, state_side, adjoint_side in zip(
        neighbours(fluid_pad), neighbours(state_pad), neighbours(adjoint_pad)
    ):
        coeff, slope = harmonic(fluid_mid, fluid_side)
        product = jnp.sum(
            (state_side - state_mid) * (adjoint_side - adjoint_mid), axis=0, keepdims=True
        )
        total = total + slope * product
    return -RELAX_RATE * total


def extend(field):
    layered = extended(field, (("rad", 1),), 1, False)
    beside_all = extended(layered, (("lon", 2),), 1, True)
    return jnp.pad(beside_all, ((0, 0), (0, 0), (0, 0), (1, 1)))


def cell_features(lon_index, lat_index, total_lon, total_lat):
    theta = math.pi * (lat_index.astype(jnp.float32) + 0.5) / total_lat
    phi = 2.0 * math.pi * lon_index.astype(jnp.float32) / total_lon
    upward = jnp.broadcast_to(jnp.cos(theta)[None, :], (phi.shape[0], theta.shape[0]))
    eastern = jnp.sin(theta)[None, :] * jnp.cos(phi)[:, None]
    northern = jnp.sin(theta)[None, :] * jnp.sin(phi)[:, None]
    return jnp.stack([upward, eastern, northern]).reshape(3, -1)


def site_features(cells, total_lon, total_lat):
    lon_index = cells // total_lat
    lat_index = cells % total_lat
    theta = math.pi * (lat_index.astype(jnp.float32) + 0.5) / total_lat
    phi = 2.0 * math.pi * lon_index.astype(jnp.float32) / total_lon
    return jnp.stack(
        [jnp.cos(theta), jnp.sin(theta) * jnp.cos(phi), jnp.sin(theta) * jnp.sin(phi)], axis=1
    )


def kernel(site_feats, cell_feats):
    cosine = (
        site_feats[:, 0:1] * cell_feats[0:1]
        + site_feats[:, 1:2] * cell_feats[1:2]
        + site_feats[:, 2:3] * cell_feats[2:3]
    )
    chord = 2.0 - 2.0 * cosine
    return 1.0 / (1.0 + chord / KERNEL_WIDTH) + 0.5 * jnp.cos(KERNEL_WAVE * chord)


def group_size(total_rows, unit, cells):
    blocks = total_rows // unit
    chosen = 1
    for candidate in range(1, 9):
        if blocks % candidate == 0 and candidate * unit * cells <= 1048576:
            chosen = candidate
    return chosen * unit


def predict_rows(feats, cell_feats, surface_flat, unit):
    size = group_size(feats.shape[0], unit, cell_feats.shape[1])
    blocks = feats.reshape(-1, size, 3)

    def one_block(block):
        weights = kernel(block, cell_feats)
        return jnp.einsum(
            "sm,cm->sc",
            weights,
            surface_flat,
            precision=lax.Precision.HIGHEST,
            preferred_element_type=jnp.float32,
        )

    return lax.map(one_block, blocks).reshape(-1, 3)


def body(
    logvisc, momentum, displacement, ice_history, load_steps, site_cells, observed, site_weight
):
    rad_rows = logvisc.shape[0]
    lon_cols = logvisc.shape[1]
    lat_cells = logvisc.shape[2]
    site_rows = site_cells.shape[0]
    total_rad = rad_rows * lax.axis_size("rad")
    total_lon = lon_cols * lax.axis_size("lon")
    lat_width = lat_cells // lax.axis_size("rad")
    scale = 1.0 / math.sqrt(total_lon * lat_cells)
    rad_global = lax.axis_index("rad") * rad_rows + jnp.arange(rad_rows)
    lon_global = lax.axis_index("lon") * lon_cols + jnp.arange(lon_cols)
    depth_weight = jnp.exp(4.0 * (rad_global.astype(jnp.float32) - (total_rad - 1)) / total_rad)
    top_row = (rad_global == total_rad - 1).astype(jnp.float32)[None, :, None, None]
    upward = (jnp.arange(3) == 0).astype(jnp.float32)[:, None, None, None]
    fluidity = jnp.exp(-logvisc)
    fluid_pad = extend(fluidity[None])
    state = displacement
    saved = []
    for level in range(RELAX):
        padded = extend(state)
        saved.append(padded)
        load = lax.dynamic_index_in_dim(ice_history, load_steps[level], 0, keepdims=False)
        state = (
            state
            + RELAX_RATE * apply_operator(padded, fluid_pad)
            - LOAD_FACTOR * upward * top_row * load[None, None]
        )
    column = jnp.sum(depth_weight[None, :, None, None] * state, axis=1)
    lat_start = lax.axis_index("rad") * lat_width
    lat_band = lat_start + jnp.arange(lat_width)
    whole_column = lax.psum(column, "rad")
    band = lax.dynamic_slice_in_dim(whole_column, lat_start, lat_width, 2)
    band_feats = cell_features(lon_global, lat_band, total_lon, lat_cells)
    own_feats = site_features(site_cells, total_lon, lat_cells)
    all_feats = lax.all_gather(own_feats, "lon", axis=0, tiled=True)
    band_flat = band.reshape(3, -1)
    partial_pred = lax.psum_scatter(
        predict_rows(all_feats, band_feats, band_flat, site_rows) * scale,
        "lon",
        scatter_dimension=0,
        tiled=True,
    )
    predicted = lax.psum(partial_pred, "rad").T
    weighted = site_weight * (predicted - observed)
    misfit = lax.psum(jnp.sum(weighted * weighted), "lon") / (3 * total_lon // lon_cols * site_rows)
    adjoint_cells = cell_features(lon_global, jnp.arange(lat_cells), total_lon, lat_cells)
    packet = jnp.concatenate([own_feats, (site_weight * weighted).T], axis=1)
    piece = lax.all_gather(packet, "lon", axis=0, tiled=True)
    size = group_size(piece.shape[0], site_rows, adjoint_cells.shape[1])
    blocks = piece.reshape(-1, size, 6)

    def add_block(running, block):
        weights = kernel(block[:, :3], adjoint_cells)
        return (
            running
            + jnp.einsum(
                "sc,sm->cm",
                block[:, 3:],
                weights,
                precision=lax.Precision.HIGHEST,
                preferred_element_type=jnp.float32,
            ),
            None,
        )

    running, unused = lax.scan(
        add_block, jnp.zeros((3, adjoint_cells.shape[1]), jnp.float32), blocks
    )
    surface_adjoint = (running * scale).reshape(3, lon_cols, lat_cells)
    adjoint = depth_weight[None, :, None, None] * surface_adjoint[:, None]
    gradient_fluid = jnp.zeros((1, rad_rows, lon_cols, lat_cells), jnp.float32)
    for level in range(RELAX - 1, -1, -1):
        adjoint_pad = extend(adjoint)
        gradient_fluid = gradient_fluid + fluid_gradient(saved[level], adjoint_pad, fluid_pad)
        if level > 0:
            adjoint = adjoint + RELAX_RATE * apply_operator(adjoint_pad, fluid_pad)
    gradient = -fluidity * gradient_fluid[0] + PRIOR_WEIGHT * logvisc
    half_momentum = momentum - 0.5 * gradient
    new_logvisc = logvisc + half_momentum
    return (new_logvisc, half_momentum, misfit.reshape(1))


def solution(mesh):
    return jax.shard_map(
        body,
        mesh=mesh,
        in_specs=(
            P("rad", "lon", None),
            P("rad", "lon", None),
            P(None, "rad", "lon", None),
            P(None, "lon", None),
            P(),
            P("lon"),
            P(None, "lon"),
            P(None, "lon"),
        ),
        out_specs=(P("rad", "lon", None), P("rad", "lon", None), P()),
        check_vma=False,
    )
```

profile of v0, /device:TPU:6, one launch (start us, length us, event | category | flops | bytes accessed | tf_op | source)
XLA Modules:
  0.0 1209.8 jit_solution(8901349295984895374)
XLA Ops:
  1.4 15.6 %collective-permute-start.3 = (f32[3,1,4,512]{3,2,1,0:T(4,128)S(1)}, f32[3,1,4,512]{3,2,1,0:T(4,128)S(1)}, u32[]{:S(2)}, u32[]{:S(2)}) collective-permute-start(f32[3,1,4,512]{3,2,1,0:T(4,128)S(1)} %get-tuple-element.153), channel_id=1, source_target_pairs={{0,1},{1,2},{2,3},{3,4},{4,5},{5,6},{6,7},{8,9},{9,10},{10,11},{11... | collective-permute-start | bytes 73736 | tf_op jit(solution)/shard_map/ppermute | solution.py:22
  17.1 1.9 collective-permute-start.1
  19.1 14.9 %collective-permute-start.2 = (f32[1,1,4,512]{3,2,1,0:T(4,128)S(1)}, f32[1,1,4,512]{3,2,1,0:T(4,128)S(1)}, u32[]{:S(2)}, u32[]{:S(2)}) collective-permute-start(f32[1,1,4,512]{3,2,1,0:T(4,128)S(1)} %get-tuple-element.163), channel_id=1, source_target_pairs={{0,1},{1,2},{2,3},{3,4},{4,5},{5,6},{6,7},{8,9},{9,10},{10,11},{11... | collective-permute-start | bytes 24584 | tf_op jit(solution)/shard_map/ppermute | solution.py:22
  34.0 1.9 collective-permute-start
  42.3 1.3 dynamic-slice_bitcast_fusion
  44.2 6.1 collective-permute-done
  50.4 1.9 collective-permute-start.6
  52.3 12.4 %collective-permute-start.4 = (f32[1,14,1,512]{3,2,1,0:T(1,128)S(1)}, f32[1,14,1,512]{3,2,1,0:T(1,128)S(1)}, u32[]{:S(2)}, u32[]{:S(2)}) collective-permute-start(f32[1,14,1,512]{3,2,1,0:T(1,128)S(1)} %get-tuple-element.160), channel_id=1, source_target_pairs={{8,0},{16,8},{24,16},{32,24},{40,32},{48,40},{56,48},{64,56},{72,6... | collective-permute-start | bytes 86024 | tf_op jit(solution)/shard_map/ppermute | solution.py:25
  65.0 1.9 collective-permute-start.7
  66.9 12.4 %collective-permute-start.5 = (f32[3,14,1,512]{3,2,1,0:T(1,128)S(1)}, f32[3,14,1,512]{3,2,1,0:T(1,128)S(1)}, u32[]{:S(2)}, u32[]{:S(2)}) collective-permute-start(f32[3,14,1,512]{3,2,1,0:T(1,128)S(1)} %get-tuple-element.146), channel_id=1, source_target_pairs={{8,0},{16,8},{24,16},{32,24},{40,32},{48,40},{56,48},{64,56},{72,6... | collective-permute-start | bytes 258056 | tf_op jit(solution)/shard_map/ppermute | solution.py:25
  83.3 8.5 collective-permute-start.9
  91.8 1.9 collective-permute-start.8
  93.8 112.6 %all-gather = f32[64,12,3]{1,2,0:T(4,128)S(1)} all-gather(f32[1,12,3]{1,2,0:T(4,128)S(1)} %maximum_bitcast_fusion.1), channel_id=1, replica_groups=mesh['lon'=64,'rad'=8] {'lon'}, dimensions={0}, use_global_device_ids=true | all-gather | bytes 9360 | tf_op jit(solution)/shard_map/all_gather | solution.py:175
  207.1 1.3 dynamic-slice
  209.6 2.2 collective-permute-start.11
  211.8 12.0 collective-permute-start.10
  224.1 1.8 collective-permute-done.10
  225.9 1.6 select_maximum_fusion.8
  227.6 1.5 multiply_reduce_fusion.6
  229.1 65.8 %psum.21 = f32[3,4,512]{2,1,0:T(4,128)S(1)} all-reduce(f32[3,4,512]{2,1,0:T(4,128)} %multiply_reduce_fusion.6), channel_id=1, replica_groups=mesh['lon'=64,'rad'=8] {'rad'}, use_global_device_ids=true, to_apply=%region_1.2 | all-reduce | flops 6144 | bytes 49152 | tf_op jit(solution)/shard_map/psum | solution.py:171
  295.6 11.0 while.21
  306.8 422.6 %all-reduce.5 = f32[768,3]{0,1:T(4,128)S(1)} all-reduce(f32[768,3]{0,1:T(4,128)S(1)} %mul.762), channel_id=2, replica_groups=mesh['lon'=64,'rad'=8] {'lon'}, use_global_device_ids=true, to_apply=%region_4.5.clone | all-reduce | flops 2304 | bytes 18432
  729.5 35.5 %psum.22 = f32[3,12]{1,0:T(4,128)S(1)} all-reduce(f32[3,12]{1,0:T(4,128)S(1)} %dynamic-slice_bitcast_fusion.2), channel_id=1, replica_groups=mesh['lon'=64,'rad'=8] {'rad'}, use_global_device_ids=true, to_apply=%region_5.6 | all-reduce | flops 36 | bytes 288 | tf_op jit(solution)/shard_map/psum | solution.py:183
  766.3 113.3 %all-gather.1 = f32[64,12,6]{1,2,0:T(8,128)S(1)} all-gather(f32[1,12,6]{1,2,0:T(8,128)S(1)} %maximum_bitcast_fusion), channel_id=1, replica_groups=mesh['lon'=64,'rad'=8] {'lon'}, dimensions={0}, use_global_device_ids=true | all-gather | bytes 18720 | tf_op jit(solution)/shard_map/all_gather | solution.py:188
  880.4 28.1 %while.22 = (s32[]{:T(128)}, f32[3,2048]{1,0:T(4,128)S(1)}, f32[8,96,6]{1,0,2:T(8,128)S(1)}, f32[3,2048]{1,0:T(4,128)S(1)}, s32[]{:T(128)}, /*index=5*/s32[]{:T(128)}) while((s32[]{:T(128)}, f32[3,2048]{1,0:T(4,128)S(1)}, f32[8,96,6]{1,0,2:T(8,128)S(1)}, f32[3,2048]{1,0:T(4,128)S(1)}, s32[]{:T(128)}, /*index=5*/s32[]{:T(128)}) %tuple.102), condition=%wide.region_7.8_spmd.clone, body=%wide.region_6.7_spmd.clone.sunk | while | flops 9646083 | bytes 146267 | solution.py:206
  880.5 3.4 convolution_add_fusion.2
  884.0 3.4 convolution_add_fusion.2
  887.5 3.4 convolution_add_fusion.2
  891.0 3.4 convolution_add_fusion.2
  894.5 3.4 convolution_add_fusion.2
  898.0 3.4 convolution_add_fusion.2
  901.6 3.4 convolution_add_fusion.2
  905.1 3.4 convolution_add_fusion.2
  909.4 12.8 %collective-permute-start.13 = (f32[3,1,4,512]{3,2,1,0:T(4,128)S(1)}, f32[3,1,4,512]{3,2,1,0:T(4,128)S(1)}, u32[]{:S(2)}, u32[]{:S(2)}) collective-permute-start(f32[3,1,4,512]{3,2,1,0:T(4,128)S(1)} %get-tuple-element.149), channel_id=1, source_target_pairs={{0,1},{1,2},{2,3},{3,4},{4,5},{5,6},{6,7},{8,9},{9,10},{10,11},{11... | collective-permute-start | bytes 73736 | tf_op jit(solution)/shard_map/ppermute | solution.py:22
  922.2 1.9 collective-permute-start.12
  924.1 14.6 %collective-permute-done.12 = f32[3,1,4,512]{3,2,1,0:T(4,128)S(1)} collective-permute-done((f32[3,1,4,512]{3,2,1,0:T(4,128)S(1)}, f32[3,1,4,512]{3,2,1,0:T(4,128)S(1)}, u32[]{:S(2)}, u32[]{:S(2)}) %collective-permute-start.12) | collective-permute-done | bytes 24608 | tf_op jit(solution)/shard_map/ppermute | solution.py:25
  939.5 1.9 collective-permute-start.15
  941.5 12.4 %collective-permute-start.14 = (f32[3,14,1,512]{3,2,1,0:T(1,128)}, f32[3,14,1,512]{3,2,1,0:T(1,128)}, u32[]{:S(2)}, u32[]{:S(2)}) collective-permute-start(f32[3,14,1,512]{3,2,1,0:T(1,128)} %get-tuple-element.142), channel_id=1, source_target_pairs={{8,0},{16,8},{24,16},{32,24},{40,32},{48,40},{56,48},{64,56},{72,6... | collective-permute-start | bytes 258056 | tf_op jit(solution)/shard_map/ppermute | solution.py:25
  953.8 210.9 %psum.23 = f32[]{:T(128)} all-reduce(f32[]{:T(128)} %get-tuple-element.169), channel_id=1, replica_groups=mesh['lon'=64,'rad'=8] {'lon'}, use_global_device_ids=true, to_apply=%region_21.22 | all-reduce | flops 1 | bytes 8 | tf_op jit(solution)/shard_map/psum | solution.py:185
  1165.4 1.9 select_maximum_fusion.4
  1167.4 1.7 multiply_add_fusion
  1169.1 1.9 collective-permute-start.17
  1171.1 3.9 collective-permute-start.16
  1175.9 11.7 collective-permute-done.16
  1187.7 1.9 collective-permute-start.19
  1189.7 12.5 %collective-permute-start.18 = (f32[3,14,1,512]{3,2,1,0:T(1,128)S(1)}, f32[3,14,1,512]{3,2,1,0:T(1,128)S(1)}, u32[]{:S(2)}, u32[]{:S(2)}) collective-permute-start(f32[3,14,1,512]{3,2,1,0:T(1,128)S(1)} %get-tuple-element.140), channel_id=1, source_target_pairs={{8,0},{16,8},{24,16},{32,24},{40,32},{48,40},{56,48},{64,56},{72,6... | collective-permute-start | bytes 258056 | tf_op jit(solution)/shard_map/ppermute | solution.py:25
  1202.2 1.7 multiply_reduce_fusion.3
  1207.4 1.2 fusion.134
  (283 shorter events, 29.9 us)
Async XLA Ops:
  0.6 18.4 %copy-start.10 = (f32[12,4,512]{2,1,0:T(4,128)S(1)}, f32[12,4,512]{2,1,0:T(4,128)}, u32[]{:S(2)}) copy-start(f32[12,4,512]{2,1,0:T(4,128)} %param.12) | copy-start | bytes 294916
  1.4 63.3 %collective-permute-start.3 = (f32[3,1,4,512]{3,2,1,0:T(4,128)S(1)}, f32[3,1,4,512]{3,2,1,0:T(4,128)S(1)}, u32[]{:S(2)}, u32[]{:S(2)}) collective-permute-start(f32[3,1,4,512]{3,2,1,0:T(4,128)S(1)} %get-tuple-element.153), channel_id=1, source_target_pairs={{0,1},{1,2},{2,3},{3,4},{4,5},{5,6},{6,7},{8,9},{9,10},{10,11},{11... | collective-permute-start | bytes 73736 | tf_op jit(solution)/shard_map/ppermute | solution.py:22
  17.1 47.7 %collective-permute-start.1 = (f32[3,1,4,512]{3,2,1,0:T(4,128)S(1)}, f32[3,1,4,512]{3,2,1,0:T(4,128)S(1)}, u32[]{:S(2)}, u32[]{:S(2)}) collective-permute-start(f32[3,1,4,512]{3,2,1,0:T(4,128)S(1)} %get-tuple-element.154), channel_id=1, source_target_pairs={{1,0},{2,1},{3,2},{4,3},{5,4},{6,5},{7,6},{9,8},{10,9},{11,10},{12... | collective-permute-start | bytes 73736 | tf_op jit(solution)/shard_map/ppermute | solution.py:25
  19.1 16.9 %copy-start.55 = (s32[2]{0:T(128)S(1)}, s32[2]{0:T(128)}, u32[]{:S(2)}) copy-start(s32[2]{0:T(128)} %param.16) | copy-start | bytes 28
  19.1 20.3 %copy-start.60 = (s32[12]{0:T(128)S(1)}, s32[12]{0:T(128)}, u32[]{:S(2)}) copy-start(s32[12]{0:T(128)} %param.17) | copy-start | bytes 148
  19.1 45.6 %copy-start = (f32[3,12,4,512]{3,2,1,0:T(4,128)S(1)}, f32[3,12,4,512]{3,2,1,0:T(4,128)}, u32[]{:S(2)}) copy-start(f32[3,12,4,512]{3,2,1,0:T(4,128)} %param.14) | copy-start | bytes 884740
  19.1 25.1 %collective-permute-start.2 = (f32[1,1,4,512]{3,2,1,0:T(4,128)S(1)}, f32[1,1,4,512]{3,2,1,0:T(4,128)S(1)}, u32[]{:S(2)}, u32[]{:S(2)}) collective-permute-start(f32[1,1,4,512]{3,2,1,0:T(4,128)S(1)} %get-tuple-element.163), channel_id=1, source_target_pairs={{0,1},{1,2},{2,3},{3,4},{4,5},{5,6},{6,7},{8,9},{9,10},{10,11},{11... | collective-permute-start | bytes 24584 | tf_op jit(solution)/shard_map/ppermute | solution.py:22
  34.0 16.4 %collective-permute-start = (f32[1,1,4,512]{3,2,1,0:T(4,128)S(1)}, f32[1,1,4,512]{3,2,1,0:T(4,128)S(1)}, u32[]{:S(2)}, u32[]{:S(2)}) collective-permute-start(f32[1,1,4,512]{3,2,1,0:T(4,128)S(1)} %get-tuple-element.164), channel_id=1, source_target_pairs={{1,0},{2,1},{3,2},{4,3},{5,4},{6,5},{7,6},{9,8},{10,9},{11,10},{12... | collective-permute-start | bytes 24584 | tf_op jit(solution)/shard_map/ppermute | solution.py:25
  39.4 54.3 %copy-start.56 = (f32[12,1]{0,1:T(1,128)}, f32[12,1]{0,1:T(1,128)S(1)}, u32[]{:S(2)}) copy-start(f32[12,1]{0,1:T(1,128)S(1)} %get-tuple-element.121) | copy-start | bytes 148
  39.5 54.2 %copy-start.51 = (f32[12,1]{0,1:T(1,128)}, f32[12,1]{0,1:T(1,128)S(1)}, u32[]{:S(2)}) copy-start(f32[12,1]{0,1:T(1,128)S(1)} %get-tuple-element.123) | copy-start | bytes 148
  39.5 54.2 %copy-start.58 = (f32[12,1]{0,1:T(1,128)}, f32[12,1]{0,1:T(1,128)S(1)}, u32[]{:S(2)}) copy-start(f32[12,1]{0,1:T(1,128)S(1)} %multiply_bitcast_fusion.1) | copy-start | bytes 148
  40.3 42.0 %copy-start.46 = (f32[3,12]{1,0:T(4,128)}, f32[3,12]{1,0:T(4,128)S(1)}, u32[]{:S(2)}) copy-start(f32[3,12]{1,0:T(4,128)S(1)} %broadcast_multiply_fusion.3) | copy-start | bytes 436
  44.2 35.4 %copy-start.38 = (f32[1,1,4,512]{3,2,1,0:T(4,128)}, f32[1,1,4,512]{3,2,1,0:T(4,128)S(1)}, u32[]{:S(2)}) copy-start(f32[1,1,4,512]{3,2,1,0:T(4,128)S(1)} %collective-permute-done.2) | copy-start | bytes 24580
  50.4 29.3 %copy-start.40 = (f32[1,1,4,512]{3,2,1,0:T(4,128)}, f32[1,1,4,512]{3,2,1,0:T(4,128)S(1)}, u32[]{:S(2)}) copy-start(f32[1,1,4,512]{3,2,1,0:T(4,128)S(1)} %collective-permute-done) | copy-start | bytes 24580
  50.4 28.9 %collective-permute-start.6 = (f32[1,14,1,512]{3,2,1,0:T(1,128)S(1)}, f32[1,14,1,512]{3,2,1,0:T(1,128)S(1)}, u32[]{:S(2)}, u32[]{:S(2)}) collective-permute-start(f32[1,14,1,512]{3,2,1,0:T(1,128)S(1)} %get-tuple-element.159), channel_id=1, source_target_pairs={{0,8},{8,16},{16,24},{24,32},{32,40},{40,48},{48,56},{56,64},{64,7... | collective-permute-start | bytes 86024 | tf_op jit(solution)/shard_map/ppermute | solution.py:22
  52.3 26.9 %collective-permute-start.4 = (f32[1,14,1,512]{3,2,1,0:T(1,128)S(1)}, f32[1,14,1,512]{3,2,1,0:T(1,128)S(1)}, u32[]{:S(2)}, u32[]{:S(2)}) collective-permute-start(f32[1,14,1,512]{3,2,1,0:T(1,128)S(1)} %get-tuple-element.160), channel_id=1, source_target_pairs={{8,0},{16,8},{24,16},{32,24},{40,32},{48,40},{56,48},{64,56},{72,6... | collective-permute-start | bytes 86024 | tf_op jit(solution)/shard_map/ppermute | solution.py:25
  64.7 17.6 %copy-start.34 = (f32[3,1,4,512]{3,2,1,0:T(4,128)}, f32[3,1,4,512]{3,2,1,0:T(4,128)S(1)}, u32[]{:S(2)}) copy-start(f32[3,1,4,512]{3,2,1,0:T(4,128)S(1)} %collective-permute-done.3) | copy-start | bytes 73732
  64.8 17.6 %copy-start.36 = (f32[3,1,4,512]{3,2,1,0:T(4,128)}, f32[3,1,4,512]{3,2,1,0:T(4,128)S(1)}, u32[]{:S(2)}) copy-start(f32[3,1,4,512]{3,2,1,0:T(4,128)S(1)} %collective-permute-done.1) | copy-start | bytes 73732
  65.0 15.3 %collective-permute-start.7 = (f32[3,14,1,512]{3,2,1,0:T(1,128)S(1)}, f32[3,14,1,512]{3,2,1,0:T(1,128)S(1)}, u32[]{:S(2)}, u32[]{:S(2)}) collective-permute-start(f32[3,14,1,512]{3,2,1,0:T(1,128)S(1)} %get-tuple-element.145), channel_id=1, source_target_pairs={{0,8},{8,16},{16,24},{24,32},{32,40},{40,48},{48,56},{56,64},{64,7... | collective-permute-start | bytes 258056 | tf_op jit(solution)/shard_map/ppermute | solution.py:22
  66.9 14.6 %collective-permute-start.5 = (f32[3,14,1,512]{3,2,1,0:T(1,128)S(1)}, f32[3,14,1,512]{3,2,1,0:T(1,128)S(1)}, u32[]{:S(2)}, u32[]{:S(2)}) collective-permute-start(f32[3,14,1,512]{3,2,1,0:T(1,128)S(1)} %get-tuple-element.146), channel_id=1, source_target_pairs={{8,0},{16,8},{24,16},{32,24},{40,32},{48,40},{56,48},{64,56},{72,6... | collective-permute-start | bytes 258056 | tf_op jit(solution)/shard_map/ppermute | solution.py:25
  80.2 147.3 %copy-start.1 = (f32[12,4,512]{2,1,0:T(4,128)}, f32[12,4,512]{2,1,0:T(4,128)S(1)}, u32[]{:S(2)}) copy-start(f32[12,4,512]{2,1,0:T(4,128)S(1)} %get-tuple-element.157) | copy-start | bytes 294916
  80.2 147.3 %copy-start.3 = (f32[12,4,512]{2,1,0:T(4,128)}, f32[12,4,512]{2,1,0:T(4,128)S(1)}, u32[]{:S(2)}) copy-start(f32[12,4,512]{2,1,0:T(4,128)S(1)} %get-tuple-element.158) | copy-start | bytes 294916
  80.2 147.3 %copy-start.5 = (f32[12,4,512]{2,1,0:T(4,128)}, f32[12,4,512]{2,1,0:T(4,128)S(1)}, u32[]{:S(2)}) copy-start(f32[12,4,512]{2,1,0:T(4,128)S(1)} %get-tuple-element.161) | copy-start | bytes 294916
  83.3 125.6 %collective-permute-start.9 = (f32[3,1,4,512]{3,2,1,0:T(4,128)S(1)}, f32[3,1,4,512]{3,2,1,0:T(4,128)S(1)}, u32[]{:S(2)}, u32[]{:S(2)}) collective-permute-start(f32[3,1,4,512]{3,2,1,0:T(4,128)S(1)} %get-tuple-element.151), channel_id=1, source_target_pairs={{0,1},{1,2},{2,3},{3,4},{4,5},{5,6},{6,7},{8,9},{9,10},{10,11},{11... | collective-permute-start | bytes 73736 | tf_op jit(solution)/shard_map/ppermute | solution.py:22
  91.8 117.2 %collective-permute-start.8 = (f32[3,1,4,512]{3,2,1,0:T(4,128)S(1)}, f32[3,1,4,512]{3,2,1,0:T(4,128)S(1)}, u32[]{:S(2)}, u32[]{:S(2)}) collective-permute-start(f32[3,1,4,512]{3,2,1,0:T(4,128)S(1)} %get-tuple-element.152), channel_id=1, source_target_pairs={{1,0},{2,1},{3,2},{4,3},{5,4},{6,5},{7,6},{9,8},{10,9},{11,10},{12... | collective-permute-start | bytes 73736 | tf_op jit(solution)/shard_map/ppermute | solution.py:25
  209.0 18.6 %copy-start.25 = (f32[3,1,4,512]{3,2,1,0:T(4,128)}, f32[3,1,4,512]{3,2,1,0:T(4,128)S(1)}, u32[]{:S(2)}) copy-start(f32[3,1,4,512]{3,2,1,0:T(4,128)S(1)} %collective-permute-done.9) | copy-start | bytes 73732
  209.6 14.5 %collective-permute-start.11 = (f32[3,14,1,512]{3,2,1,0:T(1,128)S(1)}, f32[3,14,1,512]{3,2,1,0:T(1,128)S(1)}, u32[]{:S(2)}, u32[]{:S(2)}) collective-permute-start(f32[3,14,1,512]{3,2,1,0:T(1,128)S(1)} %get-tuple-element.143), channel_id=1, source_target_pairs={{0,8},{8,16},{16,24},{24,32},{32,40},{40,48},{48,56},{56,64},{64,7... | collective-permute-start | bytes 258056 | tf_op jit(solution)/shard_map/ppermute | solution.py:22
  211.8 14.1 %collective-permute-start.10 = (f32[3,14,1,512]{3,2,1,0:T(1,128)S(1)}, f32[3,14,1,512]{3,2,1,0:T(1,128)S(1)}, u32[]{:S(2)}, u32[]{:S(2)}) collective-permute-start(f32[3,14,1,512]{3,2,1,0:T(1,128)S(1)} %get-tuple-element.144), channel_id=1, source_target_pairs={{8,0},{16,8},{24,16},{32,24},{40,32},{48,40},{56,48},{64,56},{72,6... | collective-permute-start | bytes 258056 | tf_op jit(solution)/shard_map/ppermute | solution.py:25
  223.9 3.7 copy-start.8
  223.9 3.7 copy-start.28
  729.5 35.5 %copy-start.53 = (f32[3,12]{1,0:T(4,128)S(1)}, f32[3,12]{1,0:T(4,128)}, u32[]{:S(2)}) copy-start(f32[3,12]{1,0:T(4,128)} %param.19) | copy-start | bytes 436
  729.5 35.5 %copy-start.54 = (f32[3,12]{1,0:T(4,128)S(1)}, f32[3,12]{1,0:T(4,128)}, u32[]{:S(2)}) copy-start(f32[3,12]{1,0:T(4,128)} %param.18) | copy-start | bytes 436
  909.4 14.7 %collective-permute-start.13 = (f32[3,1,4,512]{3,2,1,0:T(4,128)S(1)}, f32[3,1,4,512]{3,2,1,0:T(4,128)S(1)}, u32[]{:S(2)}, u32[]{:S(2)}) collective-permute-start(f32[3,1,4,512]{3,2,1,0:T(4,128)S(1)} %get-tuple-element.149), channel_id=1, source_target_pairs={{0,1},{1,2},{2,3},{3,4},{4,5},{5,6},{6,7},{8,9},{9,10},{10,11},{11... | collective-permute-start | bytes 73736 | tf_op jit(solution)/shard_map/ppermute | solution.py:22
  922.2 16.5 %collective-permute-start.12 = (f32[3,1,4,512]{3,2,1,0:T(4,128)S(1)}, f32[3,1,4,512]{3,2,1,0:T(4,128)S(1)}, u32[]{:S(2)}, u32[]{:S(2)}) collective-permute-start(f32[3,1,4,512]{3,2,1,0:T(4,128)S(1)} %get-tuple-element.150), channel_id=1, source_target_pairs={{1,0},{2,1},{3,2},{4,3},{5,4},{6,5},{7,6},{9,8},{10,9},{11,10},{12... | collective-permute-start | bytes 73736 | tf_op jit(solution)/shard_map/ppermute | solution.py:25
  924.1 15.4 %copy-start.21 = (f32[3,1,4,512]{3,2,1,0:T(4,128)}, f32[3,1,4,512]{3,2,1,0:T(4,128)S(1)}, u32[]{:S(2)}) copy-start(f32[3,1,4,512]{3,2,1,0:T(4,128)S(1)} %collective-permute-done.13) | copy-start | bytes 73732
  939.5 225.9 %collective-permute-start.15 = (f32[3,14,1,512]{3,2,1,0:T(1,128)}, f32[3,14,1,512]{3,2,1,0:T(1,128)}, u32[]{:S(2)}, u32[]{:S(2)}) collective-permute-start(f32[3,14,1,512]{3,2,1,0:T(1,128)} %get-tuple-element.141), channel_id=1, source_target_pairs={{0,8},{8,16},{16,24},{24,32},{32,40},{40,48},{48,56},{56,64},{64,7... | collective-permute-start | bytes 258056 | tf_op jit(solution)/shard_map/ppermute | solution.py:22
  941.5 224.0 %collective-permute-start.14 = (f32[3,14,1,512]{3,2,1,0:T(1,128)}, f32[3,14,1,512]{3,2,1,0:T(1,128)}, u32[]{:S(2)}, u32[]{:S(2)}) collective-permute-start(f32[3,14,1,512]{3,2,1,0:T(1,128)} %get-tuple-element.142), channel_id=1, source_target_pairs={{8,0},{16,8},{24,16},{32,24},{40,32},{48,40},{56,48},{64,56},{72,6... | collective-permute-start | bytes 258056 | tf_op jit(solution)/shard_map/ppermute | solution.py:25
  1169.1 5.9 copy-start.26
  1169.1 5.9 copy-start.29
  1169.1 6.8 collective-permute-start.17
  1171.1 16.5 %collective-permute-start.16 = (f32[3,1,4,512]{3,2,1,0:T(4,128)S(1)}, f32[3,1,4,512]{3,2,1,0:T(4,128)S(1)}, u32[]{:S(2)}, u32[]{:S(2)}) collective-permute-start(f32[3,1,4,512]{3,2,1,0:T(4,128)S(1)} %get-tuple-element.148), channel_id=1, source_target_pairs={{1,0},{2,1},{3,2},{4,3},{5,4},{6,5},{7,6},{9,8},{10,9},{11,10},{12... | collective-permute-start | bytes 73736 | tf_op jit(solution)/shard_map/ppermute | solution.py:25
  1175.9 26.3 %copy-start.13 = (f32[3,14,1,512]{3,2,1,0:T(1,128)S(1)}, f32[3,14,1,512]{3,2,1,0:T(1,128)}, u32[]{:S(2)}) copy-start(f32[3,14,1,512]{3,2,1,0:T(1,128)} %copy-done.12) | copy-start | bytes 258052
  1175.9 26.3 %copy-start.15 = (f32[3,14,1,512]{3,2,1,0:T(1,128)S(1)}, f32[3,14,1,512]{3,2,1,0:T(1,128)}, u32[]{:S(2)}) copy-start(f32[3,14,1,512]{3,2,1,0:T(1,128)} %copy-done.14) | copy-start | bytes 258052
  1187.7 16.2 %collective-permute-start.19 = (f32[3,14,1,512]{3,2,1,0:T(1,128)S(1)}, f32[3,14,1,512]{3,2,1,0:T(1,128)S(1)}, u32[]{:S(2)}, u32[]{:S(2)}) collective-permute-start(f32[3,14,1,512]{3,2,1,0:T(1,128)S(1)} %get-tuple-element.139), channel_id=1, source_target_pairs={{0,8},{8,16},{16,24},{24,32},{32,40},{40,48},{48,56},{56,64},{64,7... | collective-permute-start | bytes 258056 | tf_op jit(solution)/shard_map/ppermute | solution.py:22
  1189.7 14.6 %copy-start.17 = (f32[3,14,1,512]{3,2,1,0:T(1,128)S(1)}, f32[3,14,1,512]{3,2,1,0:T(1,128)}, u32[]{:S(2)}) copy-start(f32[3,14,1,512]{3,2,1,0:T(1,128)} %copy-done.16) | copy-start | bytes 258052
  1189.7 14.6 %copy-start.19 = (f32[3,14,1,512]{3,2,1,0:T(1,128)S(1)}, f32[3,14,1,512]{3,2,1,0:T(1,128)}, u32[]{:S(2)}) copy-start(f32[3,14,1,512]{3,2,1,0:T(1,128)} %copy-done.18) | copy-start | bytes 258052
  1189.7 14.6 %copy-start.37 = (f32[3,1,4,512]{3,2,1,0:T(4,128)S(1)}, f32[3,1,4,512]{3,2,1,0:T(4,128)}, u32[]{:S(2)}) copy-start(f32[3,1,4,512]{3,2,1,0:T(4,128)} %copy-done.36) | copy-start | bytes 73732
  1189.7 14.6 %collective-permute-start.18 = (f32[3,14,1,512]{3,2,1,0:T(1,128)S(1)}, f32[3,14,1,512]{3,2,1,0:T(1,128)S(1)}, u32[]{:S(2)}, u32[]{:S(2)}) collective-permute-start(f32[3,14,1,512]{3,2,1,0:T(1,128)S(1)} %get-tuple-element.140), channel_id=1, source_target_pairs={{8,0},{16,8},{24,16},{32,24},{40,32},{48,40},{56,48},{64,56},{72,6... | collective-permute-start | bytes 258056 | tf_op jit(solution)/shard_map/ppermute | solution.py:25
  (33 other events, 46.6 us)
where the time goes:
time: 1210 us
  blocking collectives  961 us (79%)
  starting transfers between devices  137 us (11%)
  waiting for transfers between devices  36.1 us (3%)
  matrix products  32.3 us (3%)
  other arithmetic  19.4 us (2%)
  local copies, waits for them, and re-layouts  16 us (1%)
    unnamed x1, blocking collectives  423 us
    psum x1, blocking collectives, body(): lax.psum(jnp.sum(weighted * weighted), 'lon')  211 us
    all_gather x1, blocking collectives, body(): piece = lax.all_gather(packet, 'lon', axis=0, tiled=True)  113 us
    all_gather x1, blocking collectives, body(): all_feats = lax.all_gather(own_feats, 'lon', axis=0, tiled=True)  113 us
    ppermute x10, starting transfers between devices, extended(): lax.ppermute(lax.slice_in_dim(block, 0, width, axis=dim), axis, backward)  73.2 us
    psum x1, blocking collectives, body(): whole_column = lax.psum(column, 'rad')  65.8 us
    ppermute x10, starting transfers between devices, extended(): lax.ppermute(lax.slice_in_dim(block, block.shape[dim] - width, None, axis...  63.6 us
    ppermute x10, waiting for transfers between devices, extended(): lax.ppermute(lax.slice_in_dim(block, 0, width, axis=dim), axis, backward)  35.9 us
  transfers between devices with their start and end apart: 20, of which 7 were waited for; matrix products, arithmetic and copies ran while one was open for 1% of the time, Pallas kernels for 0%

commit v1 on v0

--- a/solution.py
+++ b/solution.py
@@ -1,3 +1,4 @@
+import functools
 import math
 import jax
 import jax.numpy as jnp
@@ -10,6 +11,16 @@
 KERNEL_WAVE = 40.0
 PRIOR_WEIGHT = 0.1
 LOAD_FACTOR = 1.0
+
+
+def view_pipes(patch, d_out):
+    b_next = lax.axis_size("lon")
+    e_now = jnp.stack(b_next * [patch], 0)
+    out_arr = lax.all_to_all(e_now, "lon", 0, 0)
+    return jnp.concatenate(out_arr, d_out)
+
+
+copies_store = functools.partial(view_pipes, d_out=0)
 
 
 def extended(block, sides, width, periodic):
@@ -185,7 +196,7 @@
     misfit = lax.psum(jnp.sum(weighted * weighted), "lon") / (3 * total_lon // lon_cols * site_rows)
     adjoint_cells = cell_features(lon_global, jnp.arange(lat_cells), total_lon, lat_cells)
     packet = jnp.concatenate([own_feats, (site_weight * weighted).T], axis=1)
-    piece = lax.all_gather(packet, "lon", axis=0, tiled=True)
+    piece = copies_store(packet)
     size = group_size(piece.shape[0], site_rows, adjoint_cells.shape[1])
     blocks = piece.reshape(-1, size, 6)
 

time: 1210 us -> 1130 us (0.934)
  blocking collectives: 961 us -> 847 us
  waiting for transfers between devices: 36.1 us -> 56.1 us
    all_gather x1 -> x0, blocking collectives: 113 us -> none  [body(): piece = lax.all_gather(packet, 'lon', axis=0, tiled=True)]
    all_to_all x0 -> x1, waiting for transfers between devices: none -> 19.8 us  [view_pipes(): out_arr = lax.all_to_all(e_now, 'lon', 0, 0)]
  transfers between devices with their start and end apart: 20 -> 21, of which waited for: 7 -> 8; matrix products, arithmetic and copies ran while one was open for 1% -> 1% of each run, Pallas kernels for 0% -> 0%
where the time goes in v1:
time: 1130 us; the launch traced here: 1120 us
  blocking collectives  847 us (75%)
  starting transfers between devices  142 us (13%)
  waiting for transfers between devices  56.1 us (5%)
  matrix products  32.3 us (3%)
  other arithmetic  19.3 us (2%)
  local copies, waits for them, and re-layouts  18.4 us (2%)
    unnamed x1, blocking collectives  423 us
    psum x1, blocking collectives, body(): lax.psum(jnp.sum(weighted * weighted), 'lon')  211 us
    all_gather x1, blocking collectives, body(): all_feats = lax.all_gather(own_feats, 'lon', axis=0, tiled=True)  113 us
    ppermute x10, starting transfers between devices, extended(): lax.ppermute(lax.slice_in_dim(block, 0, width, axis=dim), axis, backward)  73.2 us
    psum x1, blocking collectives, body(): whole_column = lax.psum(column, 'rad')  65.8 us
    ppermute x10, starting transfers between devices, extended(): lax.ppermute(lax.slice_in_dim(block, block.shape[dim] - width, None, axis...  63.6 us
    ppermute x10, waiting for transfers between devices, extended(): lax.ppermute(lax.slice_in_dim(block, 0, width, axis=dim), axis, backward)  36.1 us
    psum x1, blocking collectives, body(): predicted = lax.psum(partial_pred, 'rad').T  35.4 us
  transfers between devices with their start and end apart: 21, of which 8 were waited for; matrix products, arithmetic and copies ran while one was open for 1% of the time, Pallas kernels for 0%

profile of v1, /device:TPU:6, one launch (start us, length us, event | category | flops | bytes accessed | tf_op | source)
XLA Modules:
  0.0 1123.7 jit_solution(9706725035716149146)
XLA Ops:
  1.4 15.6 %collective-permute-start.3 = (f32[3,1,4,512]{3,2,1,0:T(4,128)S(1)}, f32[3,1,4,512]{3,2,1,0:T(4,128)S(1)}, u32[]{:S(2)}, u32[]{:S(2)}) collective-permute-start(f32[3,1,4,512]{3,2,1,0:T(4,128)S(1)} %get-tuple-element.153), channel_id=1, source_target_pairs={{0,1},{1,2},{2,3},{3,4},{4,5},{5,6},{6,7},{8,9},{9,10},{10,11},{11... | collective-permute-start | bytes 73736 | tf_op jit(solution)/shard_map/ppermute | solution.py:33
  17.1 1.9 collective-permute-start.1
  19.1 14.9 %collective-permute-start.2 = (f32[1,1,4,512]{3,2,1,0:T(4,128)S(1)}, f32[1,1,4,512]{3,2,1,0:T(4,128)S(1)}, u32[]{:S(2)}, u32[]{:S(2)}) collective-permute-start(f32[1,1,4,512]{3,2,1,0:T(4,128)S(1)} %get-tuple-element.163), channel_id=1, source_target_pairs={{0,1},{1,2},{2,3},{3,4},{4,5},{5,6},{6,7},{8,9},{9,10},{10,11},{11... | collective-permute-start | bytes 24584 | tf_op jit(solution)/shard_map/ppermute | solution.py:33
  34.0 1.9 collective-permute-start
  42.3 1.3 dynamic-slice_bitcast_fusion
  44.2 6.2 collective-permute-done
  50.4 1.9 collective-permute-start.6
  52.3 12.4 %collective-permute-start.4 = (f32[1,14,1,512]{3,2,1,0:T(1,128)S(1)}, f32[1,14,1,512]{3,2,1,0:T(1,128)S(1)}, u32[]{:S(2)}, u32[]{:S(2)}) collective-permute-start(f32[1,14,1,512]{3,2,1,0:T(1,128)S(1)} %get-tuple-element.160), channel_id=1, source_target_pairs={{8,0},{16,8},{24,16},{32,24},{40,32},{48,40},{56,48},{64,56},{72,6... | collective-permute-start | bytes 86024 | tf_op jit(solution)/shard_map/ppermute | solution.py:36
  65.0 1.9 collective-permute-start.7
  66.9 12.4 %collective-permute-start.5 = (f32[3,14,1,512]{3,2,1,0:T(1,128)S(1)}, f32[3,14,1,512]{3,2,1,0:T(1,128)S(1)}, u32[]{:S(2)}, u32[]{:S(2)}) collective-permute-start(f32[3,14,1,512]{3,2,1,0:T(1,128)S(1)} %get-tuple-element.146), channel_id=1, source_target_pairs={{8,0},{16,8},{24,16},{32,24},{40,32},{48,40},{56,48},{64,56},{72,6... | collective-permute-start | bytes 258056 | tf_op jit(solution)/shard_map/ppermute | solution.py:36
  83.3 8.4 collective-permute-start.9
  91.7 1.9 collective-permute-start.8
  94.3 112.6 %all-gather = f32[64,12,3]{1,2,0:T(4,128)S(1)} all-gather(f32[1,12,3]{1,2,0:T(4,128)S(1)} %maximum_bitcast_fusion), channel_id=1, replica_groups=mesh['lon'=64,'rad'=8] {'lon'}, dimensions={0}, use_global_device_ids=true | all-gather | bytes 9360 | tf_op jit(solution)/shard_map/all_gather | solution.py:186
  207.6 1.3 dynamic-slice
  210.3 2.2 collective-permute-start.11
  212.5 12.0 %collective-permute-start.10 = (f32[3,14,1,512]{3,2,1,0:T(1,128)S(1)}, f32[3,14,1,512]{3,2,1,0:T(1,128)S(1)}, u32[]{:S(2)}, u32[]{:S(2)}) collective-permute-start(f32[3,14,1,512]{3,2,1,0:T(1,128)S(1)} %get-tuple-element.144), channel_id=1, source_target_pairs={{8,0},{16,8},{24,16},{32,24},{40,32},{48,40},{56,48},{64,56},{72,6... | collective-permute-start | bytes 258056 | tf_op jit(solution)/shard_map/ppermute | solution.py:36
  224.8 1.9 collective-permute-done.10
  226.7 1.6 select_maximum_fusion.8
  228.3 1.5 multiply_reduce_fusion.6
  229.8 65.8 %psum.21 = f32[3,4,512]{2,1,0:T(4,128)S(1)} all-reduce(f32[3,4,512]{2,1,0:T(4,128)} %multiply_reduce_fusion.6), channel_id=1, replica_groups=mesh['lon'=64,'rad'=8] {'rad'}, use_global_device_ids=true, to_apply=%region_1.2 | all-reduce | flops 6144 | bytes 49152 | tf_op jit(solution)/shard_map/psum | solution.py:182
  296.4 11.0 while.21
  307.5 422.7 %all-reduce.5 = f32[768,3]{0,1:T(4,128)S(1)} all-reduce(f32[768,3]{0,1:T(4,128)S(1)} %mul.762), channel_id=2, replica_groups=mesh['lon'=64,'rad'=8] {'lon'}, use_global_device_ids=true, to_apply=%region_4.5.clone | all-reduce | flops 2304 | bytes 18432
  730.2 35.4 %psum.22 = f32[3,12]{1,0:T(4,128)S(1)} all-reduce(f32[3,12]{1,0:T(4,128)S(1)} %dynamic-slice_bitcast_fusion.2), channel_id=1, replica_groups=mesh['lon'=64,'rad'=8] {'rad'}, use_global_device_ids=true, to_apply=%region_5.6 | all-reduce | flops 36 | bytes 288 | tf_op jit(solution)/shard_map/psum | solution.py:194
  767.7 4.9 all-to-all-start
  772.7 19.8 %all-to-all-done = f32[64,12,6]{1,2,0:T(8,128)S(1)} async-done(((f32[64,12,6]{1,2,0:T(8,128)}), f32[64,12,6]{1,2,0:T(8,128)S(1)}, u32[]{:S(2)}, u32[]{:S(2)}) %all-to-all-start) | async-done | bytes 18464 | tf_op jit(solution)/shard_map/all_to_all | solution.py:19
  794.3 28.2 %while.22 = (s32[]{:T(128)}, f32[3,2048]{1,0:T(4,128)S(1)}, f32[8,96,6]{1,0,2:T(8,128)S(1)}, f32[3,2048]{1,0:T(4,128)S(1)}, s32[]{:T(128)}, /*index=5*/s32[]{:T(128)}) while((s32[]{:T(128)}, f32[3,2048]{1,0:T(4,128)S(1)}, f32[8,96,6]{1,0,2:T(8,128)S(1)}, f32[3,2048]{1,0:T(4,128)S(1)}, s32[]{:T(128)}, /*index=5*/s32[]{:T(128)}) %tuple.101), condition=%wide.region_7.8_spmd.clone, body=%wide.region_6.7_spmd.clone.sunk | while | flops 9646083 | bytes 146267 | solution.py:217
  794.4 3.4 convolution_add_fusion.2
  797.9 3.4 convolution_add_fusion.2
  801.4 3.4 convolution_add_fusion.2
  804.9 3.4 convolution_add_fusion.2
  808.4 3.4 convolution_add_fusion.2
  812.0 3.4 convolution_add_fusion.2
  815.5 3.4 convolution_add_fusion.2
  819.0 3.4 convolution_add_fusion.2
  823.2 12.8 %collective-permute-start.13 = (f32[3,1,4,512]{3,2,1,0:T(4,128)S(1)}, f32[3,1,4,512]{3,2,1,0:T(4,128)S(1)}, u32[]{:S(2)}, u32[]{:S(2)}) collective-permute-start(f32[3,1,4,512]{3,2,1,0:T(4,128)S(1)} %get-tuple-element.149), channel_id=1, source_target_pairs={{0,1},{1,2},{2,3},{3,4},{4,5},{5,6},{6,7},{8,9},{9,10},{10,11},{11... | collective-permute-start | bytes 73736 | tf_op jit(solution)/shard_map/ppermute | solution.py:33
  836.0 1.9 collective-permute-start.12
  838.0 14.7 %collective-permute-done.12 = f32[3,1,4,512]{3,2,1,0:T(4,128)S(1)} collective-permute-done((f32[3,1,4,512]{3,2,1,0:T(4,128)S(1)}, f32[3,1,4,512]{3,2,1,0:T(4,128)S(1)}, u32[]{:S(2)}, u32[]{:S(2)}) %collective-permute-start.12) | collective-permute-done | bytes 24608 | tf_op jit(solution)/shard_map/ppermute | solution.py:36
  853.5 1.9 collective-permute-start.15
  855.4 12.4 %collective-permute-start.14 = (f32[3,14,1,512]{3,2,1,0:T(1,128)}, f32[3,14,1,512]{3,2,1,0:T(1,128)}, u32[]{:S(2)}, u32[]{:S(2)}) collective-permute-start(f32[3,14,1,512]{3,2,1,0:T(1,128)} %get-tuple-element.142), channel_id=1, source_target_pairs={{8,0},{16,8},{24,16},{32,24},{40,32},{48,40},{56,48},{64,56},{72,6... | collective-permute-start | bytes 258056 | tf_op jit(solution)/shard_map/ppermute | solution.py:36
  867.8 210.9 %psum.23 = f32[]{:T(128)} all-reduce(f32[]{:T(128)} %get-tuple-element.169), channel_id=1, replica_groups=mesh['lon'=64,'rad'=8] {'lon'}, use_global_device_ids=true, to_apply=%region_21.22 | all-reduce | flops 1 | bytes 8 | tf_op jit(solution)/shard_map/psum | solution.py:196
  1079.4 1.9 select_maximum_fusion.4
  1081.3 1.7 multiply_add_fusion
  1083.1 1.9 collective-permute-start.17
  1085.0 3.9 collective-permute-start.16
  1089.8 11.7 %collective-permute-done.16 = f32[3,1,4,512]{3,2,1,0:T(4,128)S(1)} collective-permute-done((f32[3,1,4,512]{3,2,1,0:T(4,128)S(1)}, f32[3,1,4,512]{3,2,1,0:T(4,128)S(1)}, u32[]{:S(2)}, u32[]{:S(2)}) %collective-permute-start.16) | collective-permute-done | bytes 24608 | tf_op jit(solution)/shard_map/ppermute | solution.py:36
  1101.7 1.9 collective-permute-start.19
  1103.6 12.5 %collective-permute-start.18 = (f32[3,14,1,512]{3,2,1,0:T(1,128)S(1)}, f32[3,14,1,512]{3,2,1,0:T(1,128)S(1)}, u32[]{:S(2)}, u32[]{:S(2)}) collective-permute-start(f32[3,14,1,512]{3,2,1,0:T(1,128)S(1)} %get-tuple-element.140), channel_id=1, source_target_pairs={{8,0},{16,8},{24,16},{32,24},{40,32},{48,40},{56,48},{64,56},{72,6... | collective-permute-start | bytes 258056 | tf_op jit(solution)/shard_map/ppermute | solution.py:36
  1116.2 1.7 multiply_reduce_fusion.3
  (289 shorter events, 33.3 us)
Async XLA Ops:
  0.6 18.4 %copy-start.10 = (f32[12,4,512]{2,1,0:T(4,128)S(1)}, f32[12,4,512]{2,1,0:T(4,128)}, u32[]{:S(2)}) copy-start(f32[12,4,512]{2,1,0:T(4,128)} %param.12) | copy-start | bytes 294916
  1.4 63.3 %collective-permute-start.3 = (f32[3,1,4,512]{3,2,1,0:T(4,128)S(1)}, f32[3,1,4,512]{3,2,1,0:T(4,128)S(1)}, u32[]{:S(2)}, u32[]{:S(2)}) collective-permute-start(f32[3,1,4,512]{3,2,1,0:T(4,128)S(1)} %get-tuple-element.153), channel_id=1, source_target_pairs={{0,1},{1,2},{2,3},{3,4},{4,5},{5,6},{6,7},{8,9},{9,10},{10,11},{11... | collective-permute-start | bytes 73736 | tf_op jit(solution)/shard_map/ppermute | solution.py:33
  17.1 47.7 %collective-permute-start.1 = (f32[3,1,4,512]{3,2,1,0:T(4,128)S(1)}, f32[3,1,4,512]{3,2,1,0:T(4,128)S(1)}, u32[]{:S(2)}, u32[]{:S(2)}) collective-permute-start(f32[3,1,4,512]{3,2,1,0:T(4,128)S(1)} %get-tuple-element.154), channel_id=1, source_target_pairs={{1,0},{2,1},{3,2},{4,3},{5,4},{6,5},{7,6},{9,8},{10,9},{11,10},{12... | collective-permute-start | bytes 73736 | tf_op jit(solution)/shard_map/ppermute | solution.py:36
  19.0 16.9 %copy-start.57 = (s32[2]{0:T(128)S(1)}, s32[2]{0:T(128)}, u32[]{:S(2)}) copy-start(s32[2]{0:T(128)} %param.16) | copy-start | bytes 28
  19.0 20.3 %copy-start.62 = (s32[12]{0:T(128)S(1)}, s32[12]{0:T(128)}, u32[]{:S(2)}) copy-start(s32[12]{0:T(128)} %param.17) | copy-start | bytes 148
  19.1 45.7 %copy-start = (f32[3,12,4,512]{3,2,1,0:T(4,128)S(1)}, f32[3,12,4,512]{3,2,1,0:T(4,128)}, u32[]{:S(2)}) copy-start(f32[3,12,4,512]{3,2,1,0:T(4,128)} %param.14) | copy-start | bytes 884740
  19.1 25.1 %collective-permute-start.2 = (f32[1,1,4,512]{3,2,1,0:T(4,128)S(1)}, f32[1,1,4,512]{3,2,1,0:T(4,128)S(1)}, u32[]{:S(2)}, u32[]{:S(2)}) collective-permute-start(f32[1,1,4,512]{3,2,1,0:T(4,128)S(1)} %get-tuple-element.163), channel_id=1, source_target_pairs={{0,1},{1,2},{2,3},{3,4},{4,5},{5,6},{6,7},{8,9},{9,10},{10,11},{11... | collective-permute-start | bytes 24584 | tf_op jit(solution)/shard_map/ppermute | solution.py:33
  34.0 16.4 %collective-permute-start = (f32[1,1,4,512]{3,2,1,0:T(4,128)S(1)}, f32[1,1,4,512]{3,2,1,0:T(4,128)S(1)}, u32[]{:S(2)}, u32[]{:S(2)}) collective-permute-start(f32[1,1,4,512]{3,2,1,0:T(4,128)S(1)} %get-tuple-element.164), channel_id=1, source_target_pairs={{1,0},{2,1},{3,2},{4,3},{5,4},{6,5},{7,6},{9,8},{10,9},{11,10},{12... | collective-permute-start | bytes 24584 | tf_op jit(solution)/shard_map/ppermute | solution.py:36
  39.4 54.3 %copy-start.58 = (f32[12,1]{0,1:T(1,128)}, f32[12,1]{0,1:T(1,128)S(1)}, u32[]{:S(2)}) copy-start(f32[12,1]{0,1:T(1,128)S(1)} %get-tuple-element.121) | copy-start | bytes 148
  39.5 54.2 %copy-start.53 = (f32[12,1]{0,1:T(1,128)}, f32[12,1]{0,1:T(1,128)S(1)}, u32[]{:S(2)}) copy-start(f32[12,1]{0,1:T(1,128)S(1)} %get-tuple-element.123) | copy-start | bytes 148
  39.5 54.2 %copy-start.60 = (f32[12,1]{0,1:T(1,128)}, f32[12,1]{0,1:T(1,128)S(1)}, u32[]{:S(2)}) copy-start(f32[12,1]{0,1:T(1,128)S(1)} %multiply_bitcast_fusion.1) | copy-start | bytes 148
  40.3 42.0 %copy-start.48 = (f32[3,12]{1,0:T(4,128)}, f32[3,12]{1,0:T(4,128)S(1)}, u32[]{:S(2)}) copy-start(f32[3,12]{1,0:T(4,128)S(1)} %broadcast_multiply_fusion.3) | copy-start | bytes 436
  44.2 35.5 %copy-start.37 = (f32[1,1,4,512]{3,2,1,0:T(4,128)}, f32[1,1,4,512]{3,2,1,0:T(4,128)S(1)}, u32[]{:S(2)}) copy-start(f32[1,1,4,512]{3,2,1,0:T(4,128)S(1)} %collective-permute-done.2) | copy-start | bytes 24580
  50.4 29.3 %copy-start.39 = (f32[1,1,4,512]{3,2,1,0:T(4,128)}, f32[1,1,4,512]{3,2,1,0:T(4,128)S(1)}, u32[]{:S(2)}) copy-start(f32[1,1,4,512]{3,2,1,0:T(4,128)S(1)} %collective-permute-done) | copy-start | bytes 24580
  50.4 28.9 %collective-permute-start.6 = (f32[1,14,1,512]{3,2,1,0:T(1,128)S(1)}, f32[1,14,1,512]{3,2,1,0:T(1,128)S(1)}, u32[]{:S(2)}, u32[]{:S(2)}) collective-permute-start(f32[1,14,1,512]{3,2,1,0:T(1,128)S(1)} %get-tuple-element.159), channel_id=1, source_target_pairs={{0,8},{8,16},{16,24},{24,32},{32,40},{40,48},{48,56},{56,64},{64,7... | collective-permute-start | bytes 86024 | tf_op jit(solution)/shard_map/ppermute | solution.py:33
  52.3 26.9 %collective-permute-start.4 = (f32[1,14,1,512]{3,2,1,0:T(1,128)S(1)}, f32[1,14,1,512]{3,2,1,0:T(1,128)S(1)}, u32[]{:S(2)}, u32[]{:S(2)}) collective-permute-start(f32[1,14,1,512]{3,2,1,0:T(1,128)S(1)} %get-tuple-element.160), channel_id=1, source_target_pairs={{8,0},{16,8},{24,16},{32,24},{40,32},{48,40},{56,48},{64,56},{72,6... | collective-permute-start | bytes 86024 | tf_op jit(solution)/shard_map/ppermute | solution.py:36
  64.7 17.6 %copy-start.33 = (f32[3,1,4,512]{3,2,1,0:T(4,128)}, f32[3,1,4,512]{3,2,1,0:T(4,128)S(1)}, u32[]{:S(2)}) copy-start(f32[3,1,4,512]{3,2,1,0:T(4,128)S(1)} %collective-permute-done.3) | copy-start | bytes 73732
  64.8 17.6 %copy-start.35 = (f32[3,1,4,512]{3,2,1,0:T(4,128)}, f32[3,1,4,512]{3,2,1,0:T(4,128)S(1)}, u32[]{:S(2)}) copy-start(f32[3,1,4,512]{3,2,1,0:T(4,128)S(1)} %collective-permute-done.1) | copy-start | bytes 73732
  65.0 15.3 %collective-permute-start.7 = (f32[3,14,1,512]{3,2,1,0:T(1,128)S(1)}, f32[3,14,1,512]{3,2,1,0:T(1,128)S(1)}, u32[]{:S(2)}, u32[]{:S(2)}) collective-permute-start(f32[3,14,1,512]{3,2,1,0:T(1,128)S(1)} %get-tuple-element.145), channel_id=1, source_target_pairs={{0,8},{8,16},{16,24},{24,32},{32,40},{40,48},{48,56},{56,64},{64,7... | collective-permute-start | bytes 258056 | tf_op jit(solution)/shard_map/ppermute | solution.py:33
  66.9 14.6 %collective-permute-start.5 = (f32[3,14,1,512]{3,2,1,0:T(1,128)S(1)}, f32[3,14,1,512]{3,2,1,0:T(1,128)S(1)}, u32[]{:S(2)}, u32[]{:S(2)}) collective-permute-start(f32[3,14,1,512]{3,2,1,0:T(1,128)S(1)} %get-tuple-element.146), channel_id=1, source_target_pairs={{8,0},{16,8},{24,16},{32,24},{40,32},{48,40},{56,48},{64,56},{72,6... | collective-permute-start | bytes 258056 | tf_op jit(solution)/shard_map/ppermute | solution.py:36
  80.2 148.0 %copy-start.1 = (f32[12,4,512]{2,1,0:T(4,128)}, f32[12,4,512]{2,1,0:T(4,128)S(1)}, u32[]{:S(2)}) copy-start(f32[12,4,512]{2,1,0:T(4,128)S(1)} %get-tuple-element.157) | copy-start | bytes 294916
  80.2 148.0 %copy-start.3 = (f32[12,4,512]{2,1,0:T(4,128)}, f32[12,4,512]{2,1,0:T(4,128)S(1)}, u32[]{:S(2)}) copy-start(f32[12,4,512]{2,1,0:T(4,128)S(1)} %get-tuple-element.158) | copy-start | bytes 294916
  80.2 148.0 %copy-start.5 = (f32[12,4,512]{2,1,0:T(4,128)}, f32[12,4,512]{2,1,0:T(4,128)S(1)}, u32[]{:S(2)}) copy-start(f32[12,4,512]{2,1,0:T(4,128)S(1)} %get-tuple-element.161) | copy-start | bytes 294916
  83.3 126.3 %collective-permute-start.9 = (f32[3,1,4,512]{3,2,1,0:T(4,128)S(1)}, f32[3,1,4,512]{3,2,1,0:T(4,128)S(1)}, u32[]{:S(2)}, u32[]{:S(2)}) collective-permute-start(f32[3,1,4,512]{3,2,1,0:T(4,128)S(1)} %get-tuple-element.151), channel_id=1, source_target_pairs={{0,1},{1,2},{2,3},{3,4},{4,5},{5,6},{6,7},{8,9},{9,10},{10,11},{11... | collective-permute-start | bytes 73736 | tf_op jit(solution)/shard_map/ppermute | solution.py:33
  91.7 117.9 %collective-permute-start.8 = (f32[3,1,4,512]{3,2,1,0:T(4,128)S(1)}, f32[3,1,4,512]{3,2,1,0:T(4,128)S(1)}, u32[]{:S(2)}, u32[]{:S(2)}) collective-permute-start(f32[3,1,4,512]{3,2,1,0:T(4,128)S(1)} %get-tuple-element.152), channel_id=1, source_target_pairs={{1,0},{2,1},{3,2},{4,3},{5,4},{6,5},{7,6},{9,8},{10,9},{11,10},{12... | collective-permute-start | bytes 73736 | tf_op jit(solution)/shard_map/ppermute | solution.py:36
  209.7 18.6 %copy-start.24 = (f32[3,1,4,512]{3,2,1,0:T(4,128)}, f32[3,1,4,512]{3,2,1,0:T(4,128)S(1)}, u32[]{:S(2)}) copy-start(f32[3,1,4,512]{3,2,1,0:T(4,128)S(1)} %collective-permute-done.9) | copy-start | bytes 73732
  210.3 14.5 %collective-permute-start.11 = (f32[3,14,1,512]{3,2,1,0:T(1,128)S(1)}, f32[3,14,1,512]{3,2,1,0:T(1,128)S(1)}, u32[]{:S(2)}, u32[]{:S(2)}) collective-permute-start(f32[3,14,1,512]{3,2,1,0:T(1,128)S(1)} %get-tuple-element.143), channel_id=1, source_target_pairs={{0,8},{8,16},{16,24},{24,32},{32,40},{40,48},{48,56},{56,64},{64,7... | collective-permute-start | bytes 258056 | tf_op jit(solution)/shard_map/ppermute | solution.py:33
  212.5 14.1 %collective-permute-start.10 = (f32[3,14,1,512]{3,2,1,0:T(1,128)S(1)}, f32[3,14,1,512]{3,2,1,0:T(1,128)S(1)}, u32[]{:S(2)}, u32[]{:S(2)}) collective-permute-start(f32[3,14,1,512]{3,2,1,0:T(1,128)S(1)} %get-tuple-element.144), channel_id=1, source_target_pairs={{8,0},{16,8},{24,16},{32,24},{40,32},{48,40},{56,48},{64,56},{72,6... | collective-permute-start | bytes 258056 | tf_op jit(solution)/shard_map/ppermute | solution.py:36
  730.2 35.4 %copy-start.55 = (f32[3,12]{1,0:T(4,128)S(1)}, f32[3,12]{1,0:T(4,128)}, u32[]{:S(2)}) copy-start(f32[3,12]{1,0:T(4,128)} %param.19) | copy-start | bytes 436
  730.2 35.4 %copy-start.56 = (f32[3,12]{1,0:T(4,128)S(1)}, f32[3,12]{1,0:T(4,128)}, u32[]{:S(2)}) copy-start(f32[3,12]{1,0:T(4,128)} %param.18) | copy-start | bytes 436
  767.7 5.0 copy-start.46
  767.7 24.8 %all-to-all-start = ((f32[64,12,6]{1,2,0:T(8,128)}), f32[64,12,6]{1,2,0:T(8,128)S(1)}, u32[]{:S(2)}, u32[]{:S(2)}) async-start(f32[64,12,6]{1,2,0:T(8,128)} %stack.19), calls=%async_computation | async-start | bytes 524288 | tf_op jit(solution)/shard_map/all_to_all | solution.py:19
  823.2 14.8 %collective-permute-start.13 = (f32[3,1,4,512]{3,2,1,0:T(4,128)S(1)}, f32[3,1,4,512]{3,2,1,0:T(4,128)S(1)}, u32[]{:S(2)}, u32[]{:S(2)}) collective-permute-start(f32[3,1,4,512]{3,2,1,0:T(4,128)S(1)} %get-tuple-element.149), channel_id=1, source_target_pairs={{0,1},{1,2},{2,3},{3,4},{4,5},{5,6},{6,7},{8,9},{9,10},{10,11},{11... | collective-permute-start | bytes 73736 | tf_op jit(solution)/shard_map/ppermute | solution.py:33
  836.0 16.7 %collective-permute-start.12 = (f32[3,1,4,512]{3,2,1,0:T(4,128)S(1)}, f32[3,1,4,512]{3,2,1,0:T(4,128)S(1)}, u32[]{:S(2)}, u32[]{:S(2)}) collective-permute-start(f32[3,1,4,512]{3,2,1,0:T(4,128)S(1)} %get-tuple-element.150), channel_id=1, source_target_pairs={{1,0},{2,1},{3,2},{4,3},{5,4},{6,5},{7,6},{9,8},{10,9},{11,10},{12... | collective-permute-start | bytes 73736 | tf_op jit(solution)/shard_map/ppermute | solution.py:36
  838.0 15.5 %copy-start.20 = (f32[3,1,4,512]{3,2,1,0:T(4,128)}, f32[3,1,4,512]{3,2,1,0:T(4,128)S(1)}, u32[]{:S(2)}) copy-start(f32[3,1,4,512]{3,2,1,0:T(4,128)S(1)} %collective-permute-done.13) | copy-start | bytes 73732
  853.5 225.9 %collective-permute-start.15 = (f32[3,14,1,512]{3,2,1,0:T(1,128)}, f32[3,14,1,512]{3,2,1,0:T(1,128)}, u32[]{:S(2)}, u32[]{:S(2)}) collective-permute-start(f32[3,14,1,512]{3,2,1,0:T(1,128)} %get-tuple-element.141), channel_id=1, source_target_pairs={{0,8},{8,16},{16,24},{24,32},{32,40},{40,48},{48,56},{56,64},{64,7... | collective-permute-start | bytes 258056 | tf_op jit(solution)/shard_map/ppermute | solution.py:33
  855.4 224.0 %collective-permute-start.14 = (f32[3,14,1,512]{3,2,1,0:T(1,128)}, f32[3,14,1,512]{3,2,1,0:T(1,128)}, u32[]{:S(2)}, u32[]{:S(2)}) collective-permute-start(f32[3,14,1,512]{3,2,1,0:T(1,128)} %get-tuple-element.142), channel_id=1, source_target_pairs={{8,0},{16,8},{24,16},{32,24},{40,32},{48,40},{56,48},{64,56},{72,6... | collective-permute-start | bytes 258056 | tf_op jit(solution)/shard_map/ppermute | solution.py:36
  1083.0 5.9 copy-start.25
  1083.0 5.9 copy-start.28
  1083.1 6.8 collective-permute-start.17
  1085.0 16.5 %collective-permute-start.16 = (f32[3,1,4,512]{3,2,1,0:T(4,128)S(1)}, f32[3,1,4,512]{3,2,1,0:T(4,128)S(1)}, u32[]{:S(2)}, u32[]{:S(2)}) collective-permute-start(f32[3,1,4,512]{3,2,1,0:T(4,128)S(1)} %get-tuple-element.148), channel_id=1, source_target_pairs={{1,0},{2,1},{3,2},{4,3},{5,4},{6,5},{7,6},{9,8},{10,9},{11,10},{12... | collective-permute-start | bytes 73736 | tf_op jit(solution)/shard_map/ppermute | solution.py:36
  1089.8 26.3 %copy-start.13 = (f32[3,14,1,512]{3,2,1,0:T(1,128)S(1)}, f32[3,14,1,512]{3,2,1,0:T(1,128)}, u32[]{:S(2)}) copy-start(f32[3,14,1,512]{3,2,1,0:T(1,128)} %copy-done.12) | copy-start | bytes 258052
  1089.8 26.3 %copy-start.15 = (f32[3,14,1,512]{3,2,1,0:T(1,128)S(1)}, f32[3,14,1,512]{3,2,1,0:T(1,128)}, u32[]{:S(2)}) copy-start(f32[3,14,1,512]{3,2,1,0:T(1,128)} %copy-done.14) | copy-start | bytes 258052
  1101.7 16.2 %collective-permute-start.19 = (f32[3,14,1,512]{3,2,1,0:T(1,128)S(1)}, f32[3,14,1,512]{3,2,1,0:T(1,128)S(1)}, u32[]{:S(2)}, u32[]{:S(2)}) collective-permute-start(f32[3,14,1,512]{3,2,1,0:T(1,128)S(1)} %get-tuple-element.139), channel_id=1, source_target_pairs={{0,8},{8,16},{16,24},{24,32},{32,40},{40,48},{48,56},{56,64},{64,7... | collective-permute-start | bytes 258056 | tf_op jit(solution)/shard_map/ppermute | solution.py:33
  1103.6 14.6 %copy-start.17 = (f32[3,14,1,512]{3,2,1,0:T(1,128)S(1)}, f32[3,14,1,512]{3,2,1,0:T(1,128)}, u32[]{:S(2)}) copy-start(f32[3,14,1,512]{3,2,1,0:T(1,128)} %copy-done.16) | copy-start | bytes 258052
  1103.6 14.6 %copy-start.19 = (f32[3,14,1,512]{3,2,1,0:T(1,128)S(1)}, f32[3,14,1,512]{3,2,1,0:T(1,128)}, u32[]{:S(2)}) copy-start(f32[3,14,1,512]{3,2,1,0:T(1,128)} %copy-done.18) | copy-start | bytes 258052
  1103.6 14.6 %copy-start.36 = (f32[3,1,4,512]{3,2,1,0:T(4,128)S(1)}, f32[3,1,4,512]{3,2,1,0:T(4,128)}, u32[]{:S(2)}) copy-start(f32[3,1,4,512]{3,2,1,0:T(4,128)} %copy-done.35) | copy-start | bytes 73732
  1103.6 14.6 %collective-permute-start.18 = (f32[3,14,1,512]{3,2,1,0:T(1,128)S(1)}, f32[3,14,1,512]{3,2,1,0:T(1,128)S(1)}, u32[]{:S(2)}, u32[]{:S(2)}) collective-permute-start(f32[3,14,1,512]{3,2,1,0:T(1,128)S(1)} %get-tuple-element.140), channel_id=1, source_target_pairs={{8,0},{16,8},{24,16},{32,24},{40,32},{48,40},{56,48},{64,56},{72,6... | collective-permute-start | bytes 258056 | tf_op jit(solution)/shard_map/ppermute | solution.py:36
  (36 other events, 63.5 us)
